TPU v7x, 32 devices: a whole 2x2x4 slice. The times are simulated.
32 devices in a mesh: parts: 2 (over x), space: 16 (over z, y, core).
Axes of the slice: x: 2, y: 2, z: 4, core: 2. Of those that a mesh axis runs over, the one named last changes fastest.
Arguments:
- gas_q: bfloat16 [12288, 512], P(('parts', 'space')), parts along dimension 0, may hold values from -6 to 6
- gas_k: bfloat16 [12288, 512], P(('parts', 'space')), parts along dimension 0, may hold values from -6 to 6
- gas_v: bfloat16 [12288, 512], P(('parts', 'space')), parts along dimension 0, may hold values from -6 to 6
- gas_cotan: bfloat16 [12288, 512], P(('parts', 'space')), parts along dimension 0, may hold values from -6 to 6
- nbr_ids: int32 [96, 16], P('parts'), parts along dimension 0, may hold values from 0 to 47, as said below
- nbr_valid: int32 [96, 16], P('parts'), parts along dimension 0, may hold values from 0 to 1
- if_row: int32 [512], P(('parts', 'space')), parts along dimension 0, may hold values from 0 to 383, as said below
- if_dst: int32 [512], P(('parts', 'space')), parts along dimension 0, may hold values from 0 to 15, as said below
- melt_q: bfloat16 [4096, 512], P(('parts', 'space')), parts along dimension 0, may hold values from -6 to 6
- melt_k: bfloat16 [4096, 512], P(('parts', 'space')), parts along dimension 0, may hold values from -6 to 6
- melt_v: bfloat16 [4096, 512], P(('parts', 'space')), parts along dimension 0, may hold values from -6 to 6
- melt_cotan: bfloat16 [4096, 512], P(('parts', 'space')), parts along dimension 0, may hold values from -6 to 6
Outputs:
- gas_out: bfloat16 [12288, 512], P(('parts', 'space')), parts along dimension 0
- gas_dq: bfloat16 [12288, 512], P(('parts', 'space')), parts along dimension 0
- gas_dk: bfloat16 [12288, 512], P(('parts', 'space')), parts along dimension 0
- gas_dv: bfloat16 [12288, 512], P(('parts', 'space')), parts along dimension 0
- melt_out: bfloat16 [4096, 512], P(('parts', 'space')), parts along dimension 0
- melt_dq: bfloat16 [4096, 512], P(('parts', 'space')), parts along dimension 0
- melt_dk: bfloat16 [4096, 512], P(('parts', 'space')), parts along dimension 0
- melt_dv: bfloat16 [4096, 512], P(('parts', 'space')), parts along dimension 0
There are 2 independent parts, one for each index of `parts`. A program takes and returns all parts, laid end to end along the dimension named above; each array names one. Nothing has to cross between parts.
Inputs may be any that keep to these rules, and one draw needn't show every extreme that they name: `nbr_ids`: for every gas block b the live entries of row b name distinct blocks, b itself among them, all in gas groups within 3 of b's group. For two different gas groups r and o within 3 of each other, the live entries of the blocks of group r name exactly one block of group o. Entries that are not live name any block. `if_row`: the 16 entries of one gas group are distinct. `if_dst`: the 16 entries of one gas group name 8 melt groups, 2 entries each; some melt group is named 2 times by every gas group.
All inputs are finite; a program needn't handle non-finite values.
Results may differ from a plain program's by a relative error of at most 0.012.
The roundings to bfloat16 on the way count: a program that leaves them out, or rounds other values in their place, can miss the bound.
Values may be sent and summed in bfloat16 or wider, within the bound.
A program may use at most 128 MiB of HBM per device.

v0:
```python
import math

import jax
import jax.numpy as jnp
from jax import lax
from jax.sharding import PartitionSpec as P

HEADS = 8
HEAD_DIM = 64
BLK = 128
WIN = 3
ICAP = 2
GB_DEV = 3


MASKED_SCORE = -1e30


def shifted_2(value, axis, steps):
    count = lax.axis_size(axis)
    initial, last = (max(0, -steps), min(count, count - steps))
    return lax.ppermute(value, axis, [(source, source + steps) for source in range(initial, last)])


def attend(queries, key_rows, values, cotangent, key_mask):
    row_count = queries.shape[0]
    key_count = key_rows.shape[0]
    query_heads = queries.reshape(row_count, HEADS, HEAD_DIM)
    key_heads = key_rows.reshape(key_count, HEADS, HEAD_DIM)
    value_heads = values.reshape(key_count, HEADS, HEAD_DIM)
    cot_heads = cotangent.reshape(row_count, HEADS, HEAD_DIM)
    inv_root = 1.0 / math.sqrt(HEAD_DIM)
    wide = jnp.float32
    scores = (
        jnp.einsum("rhd,shd->hrs", query_heads, key_heads, preferred_element_type=wide) * inv_root
    )
    scores = jnp.where(key_mask[None, None, :], scores, MASKED_SCORE)
    row_max = jnp.max(scores, axis=2, keepdims=True)
    shifted = jnp.exp(scores - row_max)
    weights = shifted / jnp.sum(shifted, axis=2, keepdims=True)
    weights_low = weights.astype(jnp.bfloat16)
    attended = jnp.einsum(
        "hrs,shd->rhd", weights_low, value_heads, preferred_element_type=wide
    ).reshape(row_count, -1)
    grad_weights = jnp.einsum("rhd,shd->hrs", cot_heads, value_heads, preferred_element_type=wide)
    row_delta = jnp.sum(weights * grad_weights, axis=2, keepdims=True)
    dscore = (weights * (grad_weights - row_delta)).astype(jnp.bfloat16)
    grad_query = (
        jnp.einsum("hrs,shd->rhd", dscore, key_heads, preferred_element_type=wide).reshape(
            row_count, -1
        )
        * inv_root
    )
    grad_key = (
        jnp.einsum("hrs,rhd->shd", dscore, query_heads, preferred_element_type=wide).reshape(
            key_count, -1
        )
        * inv_root
    )
    grad_value = jnp.einsum(
        "hrs,rhd->shd", weights_low, cot_heads, preferred_element_type=wide
    ).reshape(key_count, -1)
    return (attended, grad_query, grad_key, grad_value)


def local(
    gas_q,
    gas_k,
    gas_v,
    gas_cotan,
    nbr_ids,
    nbr_valid,
    if_row,
    if_dst,
    melt_q,
    melt_k,
    melt_v,
    melt_cotan,
):
    myself = lax.axis_index("space")
    devices = lax.axis_size("space")
    width = gas_q.shape[1]
    kv_local = jnp.stack([gas_k.reshape(GB_DEV, BLK, width), gas_v.reshape(GB_DEV, BLK, width)])
    offsets = [o for o in range(-WIN, WIN + 1) if o != 0]
    arrived_list = []
    arrived_ids = [myself * GB_DEV + jnp.arange(GB_DEV, dtype=jnp.int32)]
    for offset in offsets:
        owner_dev = myself - offset
        arrived = shifted_2(kv_local, "space", offset)
        arrived_list.append(arrived)
        present = (owner_dev >= 0) & (owner_dev < devices)
        arrived_ids.append(
            jnp.where(present, owner_dev * GB_DEV + jnp.arange(GB_DEV, dtype=jnp.int32), -1)
        )
    available = jnp.concatenate([kv_local] + arrived_list, axis=1)
    available_ids = jnp.concatenate(arrived_ids)
    slot_count = available.shape[1]
    my_ids = lax.dynamic_slice_in_dim(nbr_ids, myself * GB_DEV, GB_DEV, 0)
    my_live = lax.dynamic_slice_in_dim(nbr_valid, myself * GB_DEV, GB_DEV, 0) == 1
    matches = my_ids[:, :, None] == available_ids[None, None, :]
    present_entry = jnp.any(matches, axis=2) & my_live
    slot_index = jnp.sum(jnp.where(matches, jnp.arange(slot_count), 0), axis=2)
    query_blocks = gas_q.reshape(GB_DEV, BLK, width)
    cot_blocks = gas_cotan.reshape(GB_DEV, BLK, width)

    def gas_block(grad_slots, inputs_block):
        query_rows, cot_rows, slot_row, entry_ok = inputs_block
        list_len = slot_row.shape[0]
        key_rows = jnp.take(available[0], slot_row, axis=0).reshape(list_len * BLK, width)
        value_rows = jnp.take(available[1], slot_row, axis=0).reshape(list_len * BLK, width)
        key_mask = jnp.repeat(entry_ok, BLK)
        attended, grad_query, grad_key, grad_value = attend(
            query_rows, key_rows, value_rows, cot_rows, key_mask
        )
        grad_pair = jnp.stack(
            [grad_key.reshape(list_len, BLK, width), grad_value.reshape(list_len, BLK, width)]
        )
        grad_pair = jnp.where(entry_ok[None, :, None, None], grad_pair, 0.0)
        grad_slots = grad_slots.at[:, slot_row].add(grad_pair)
        return (grad_slots, (attended.astype(jnp.bfloat16), grad_query.astype(jnp.bfloat16)))

    start_slots = jnp.zeros((2, slot_count, BLK, width), jnp.float32)
    grad_slots, (gas_att, gas_gq) = lax.scan(
        gas_block, start_slots, (query_blocks, cot_blocks, slot_index, present_entry)
    )
    own_grads = grad_slots[:, :GB_DEV]
    for number, offset in enumerate(offsets):
        outgoing = grad_slots[:, GB_DEV + number * GB_DEV : GB_DEV + (number + 1) * GB_DEV]
        returned = shifted_2(outgoing, "space", -offset)
        own_grads = own_grads + returned
    if_count = if_row.shape[0]
    entry_index = jnp.arange(if_count)
    earlier = entry_index[None, :] < entry_index[:, None]
    slot_rank = jnp.sum((if_dst[:, None] == if_dst[None, :]) & earlier, axis=1)
    slot_place = if_dst * ICAP + slot_rank
    send_keys = (
        jnp.zeros((devices * ICAP, width), jnp.bfloat16)
        .at[slot_place]
        .set(gas_k[if_row])
        .reshape(devices, ICAP, width)
    )
    send_values = (
        jnp.zeros((devices * ICAP, width), jnp.bfloat16)
        .at[slot_place]
        .set(gas_v[if_row])
        .reshape(devices, ICAP, width)
    )
    row_flag = (
        jnp.zeros((devices * ICAP,), jnp.bfloat16).at[slot_place].set(1.0).reshape(devices, ICAP)
    )
    recv_keys, recv_values, recv_flag = (
        lax.all_to_all(send_keys, "space", split_axis=0, concat_axis=0, tiled=True),
        lax.all_to_all(send_values, "space", split_axis=0, concat_axis=0, tiled=True),
        lax.all_to_all(row_flag, "space", split_axis=0, concat_axis=0, tiled=True),
    )
    melt_rows = melt_q.shape[0]
    key_rows = jnp.concatenate([melt_k, recv_keys.reshape(-1, width)], axis=0)
    value_rows = jnp.concatenate([melt_v, recv_values.reshape(-1, width)], axis=0)
    key_mask = jnp.concatenate([jnp.ones((melt_rows,), bool), recv_flag.reshape(-1) > 0])
    melt_att, melt_gq, melt_gk, melt_gv = attend(melt_q, key_rows, value_rows, melt_cotan, key_mask)
    back_keys, back_values = (
        lax.all_to_all(
            melt_gk[melt_rows:].reshape(devices, ICAP, width),
            "space",
            split_axis=0,
            concat_axis=0,
            tiled=True,
        ),
        lax.all_to_all(
            melt_gv[melt_rows:].reshape(devices, ICAP, width),
            "space",
            split_axis=0,
            concat_axis=0,
            tiled=True,
        ),
    )
    extra_keys = back_keys.reshape(-1, width)[slot_place]
    extra_values = back_values.reshape(-1, width)[slot_place]
    key_flat = own_grads[0].reshape(-1, width).at[if_row].add(extra_keys)
    value_flat = own_grads[1].reshape(-1, width).at[if_row].add(extra_values)
    low = jnp.bfloat16
    return (
        gas_att.reshape(-1, width),
        gas_gq.reshape(-1, width),
        key_flat.astype(low),
        value_flat.astype(low),
        melt_att.astype(low),
        melt_gq.astype(low),
        melt_gk[:melt_rows].astype(low),
        melt_gv[:melt_rows].astype(low),
    )


def solution(mesh):
    in_specs = (
        P(("parts", "space"), None),
        P(("parts", "space"), None),
        P(("parts", "space"), None),
        P(("parts", "space"), None),
        P("parts", None),
        P("parts", None),
        P(("parts", "space")),
        P(("parts", "space")),
        P(("parts", "space"), None),
        P(("parts", "space"), None),
        P(("parts", "space"), None),
        P(("parts", "space"), None),
    )
    out_specs = (
        P(("parts", "space"), None),
        P(("parts", "space"), None),
        P(("parts", "space"), None),
        P(("parts", "space"), None),
        P(("parts", "space"), None),
        P(("parts", "space"), None),
        P(("parts", "space"), None),
        P(("parts", "space"), None),
    )
    return jax.shard_map(local, mesh=mesh, in_specs=in_specs, out_specs=out_specs, check_vma=False)
```

profile of v0, /device:TPU:0, one launch (start us, length us, event | category | flops | bytes accessed | tf_op | source)
XLA Modules:
  0.0 592.0 jit_solution(17577238697560599775)
XLA Ops:
  16.9 6.7 %collective-permute-done = bf16[2,3,128,512]{3,2,1,0:T(8,128)(2,1)} collective-permute-done((bf16[2,3,128,512]{3,2,1,0:T(8,128)(2,1)}, bf16[2,3,128,512]{3,2,1,0:T(8,128)(2,1)}, u32[]{:S(2)}, u32[]{:S(2)}) %collective-permute-start) | collective-permute-done | bytes 786464 | tf_op jit(solution)/shard_map/ppermute | solution.py:22
  31.0 32.9 %collective-permute-done.4 = bf16[2,3,128,512]{3,2,1,0:T(8,128)(2,1)S(1)} collective-permute-done((bf16[2,3,128,512]{3,2,1,0:T(8,128)(2,1)}, bf16[2,3,128,512]{3,2,1,0:T(8,128)(2,1)S(1)}, u32[]{:S(2)}, u32[]{:S(2)}) %collective-permute-start.4) | collective-permute-done | bytes 786464 | tf_op jit(solution)/shard_map/ppermute | solution.py:22
  64.8 14.4 %collective-permute-done.5 = bf16[2,3,128,512]{3,2,1,0:T(8,128)(2,1)} collective-permute-done((bf16[2,3,128,512]{3,2,1,0:T(8,128)(2,1)}, bf16[2,3,128,512]{3,2,1,0:T(8,128)(2,1)}, u32[]{:S(2)}, u32[]{:S(2)}) %collective-permute-start.5) | collective-permute-done | bytes 786464 | tf_op jit(solution)/shard_map/ppermute | solution.py:22
  81.3 5.6 broadcast_in_dim.104
  86.9 312.1 %while.14 = (s32[]{:T(128)}, f32[2,21,128,512]{3,2,1,0:T(8,128)}, bf16[3,128,512]{2,1,0:T(8,128)(2,1)}, bf16[3,128,512]{2,1,0:T(8,128)(2,1)}, s32[3,16]{1,0:T(4,...) while((s32[]{:T(128)}, f32[2,21,128,512]{3,2,1,0:T(8,128)}, ...), condition=%wide.region_7.9_spmd, body=%wide.region_2.8_spmd.sunk | while | flops 1651705984 | bytes 253007152 | solution.py:123
  123.2 5.6 multiply_reduce_fusion.3
  134.5 5.7 fusion.110
  164.6 8.5 %fusion.108 = f32[16,2,128,512]{3,2,1,0:T(8,128)} fusion(f32[1,16,128,512]{3,2,0,1:T(8,128)} %copy.133, f32[1,16,128,512]{3,2,0,1:T(8,128)} %copy.136, pred[16]{0:T(512)(128)(4,1)S(1)} %dynamic-slice_bitcast_fusion.2), kind=kLoop, calls=%fused_computation.14.clone.1 | loop fusion | flops 4194304 | bytes 16777232 | tf_op jit(solution)/shard_map/while/body/eval_jaxpr/jit(_where)/select_n | solution.py:118
  173.0 17.5 %scatter_fusion = f32[2,21,128,512]{3,2,1,0:T(8,128)} fusion(f32[2,21,128,512]{3,2,1,0:T(8,128)} %get-tuple-element.264, s32[16]{0:T(128)S(1)} %fusion.105, f32[16,2,128,512]{3,2,1,0:T(8,128)} %fusion.108), kind=kCustom, calls=%fused_computation.6.clone.1 | custom fusion | flops 2097152 | bytes 25165888 | tf_op jit(solution)/shard_map/while/body/eval_jaxpr/scatter-add | solution.py:119
  226.9 5.6 multiply_reduce_fusion.3
  238.2 5.7 fusion.110
  268.2 8.5 %fusion.108 = f32[16,2,128,512]{3,2,1,0:T(8,128)} fusion(f32[1,16,128,512]{3,2,0,1:T(8,128)} %copy.133, f32[1,16,128,512]{3,2,0,1:T(8,128)} %copy.136, pred[16]{0:T(512)(128)(4,1)S(1)} %dynamic-slice_bitcast_fusion.2), kind=kLoop, calls=%fused_computation.14.clone.1 | loop fusion | flops 4194304 | bytes 16777232 | tf_op jit(solution)/shard_map/while/body/eval_jaxpr/jit(_where)/select_n | solution.py:118
  276.7 18.3 %scatter_fusion = f32[2,21,128,512]{3,2,1,0:T(8,128)} fusion(f32[2,21,128,512]{3,2,1,0:T(8,128)} %get-tuple-element.264, s32[16]{0:T(128)S(1)} %fusion.105, f32[16,2,128,512]{3,2,1,0:T(8,128)} %fusion.108), kind=kCustom, calls=%fused_computation.6.clone.1 | custom fusion | flops 2097152 | bytes 25165888 | tf_op jit(solution)/shard_map/while/body/eval_jaxpr/scatter-add | solution.py:119
  331.3 5.6 multiply_reduce_fusion.3
  342.7 5.7 fusion.110
  372.7 8.5 %fusion.108 = f32[16,2,128,512]{3,2,1,0:T(8,128)} fusion(f32[1,16,128,512]{3,2,0,1:T(8,128)} %copy.133, f32[1,16,128,512]{3,2,0,1:T(8,128)} %copy.136, pred[16]{0:T(512)(128)(4,1)S(1)} %dynamic-slice_bitcast_fusion.2), kind=kLoop, calls=%fused_computation.14.clone.1 | loop fusion | flops 4194304 | bytes 16777232 | tf_op jit(solution)/shard_map/while/body/eval_jaxpr/jit(_where)/select_n | solution.py:118
  381.2 17.8 %scatter_fusion = f32[2,21,128,512]{3,2,1,0:T(8,128)} fusion(f32[2,21,128,512]{3,2,1,0:T(8,128)} %get-tuple-element.264, s32[16]{0:T(128)S(1)} %fusion.105, f32[16,2,128,512]{3,2,1,0:T(8,128)} %fusion.108), kind=kCustom, calls=%fused_computation.6.clone.1 | custom fusion | flops 2097152 | bytes 25165888 | tf_op jit(solution)/shard_map/while/body/eval_jaxpr/scatter-add | solution.py:119
  399.0 7.4 %fusion.52 = (f32[2,3,128,512]{3,2,1,0:T(8,128)}, f32[2,3,128,512]{3,2,1,0:T(8,128)}, f32[2,3,128,512]{3,2,1,0:T(8,128)}, f32[2,3,128,512]{3,2,1,0:T(8,128)S(1)}...) fusion(f32[2,21,128,512]{3,2,1,0:T(8,128)} %get-tuple-element.60), kind=kLoop, calls=%fused_computation.124 | loop fusion | bytes 18874368 | tf_op jit(solution)/shard_map/slice | solution.py:128
  409.3 8.9 %all-to-all-start = ((bf16[16,1,2]{2,1,0:T(2,128)(2,1)}), bf16[16,1,2]{2,1,0:T(2,128)(2,1)S(1)}, u32[]{:S(2)}, u32[]{:S(2)}) async-start(bf16[16,1,2]{2,1,0:T(2,128)(2,1)} %all_to_all.24), calls=%async_computation | async-start | bytes 16384 | tf_op jit(solution)/shard_map/all_to_all | solution.py:154
  429.4 19.0 %all-to-all-done = bf16[16,1,2]{2,1,0:T(2,128)(2,1)S(1)} async-done(((bf16[16,1,2]{2,1,0:T(2,128)(2,1)}), bf16[16,1,2]{2,1,0:T(2,128)(2,1)S(1)}, u32[]{:S(2)}, u32[]{:S(2)}) %all-to-all-start) | async-done | bytes 96 | tf_op jit(solution)/shard_map/all_to_all | solution.py:154
  452.1 6.4 %all-to-all-done.1 = bf16[16,2,512]{2,1,0:T(2,128)(2,1)S(1)} async-done(((bf16[16,2,512]{2,1,0:T(2,128)(2,1)}), bf16[16,2,512]{2,1,0:T(2,128)(2,1)S(1)}, u32[]{:S(2)}, u32[]{:S(2)}) %all-to-all-start.1) | async-done | bytes 32800 | tf_op jit(solution)/shard_map/all_to_all | solution.py:152
  469.1 5.8 collective-permute-start.7
  510.4 58.3 %all-to-all-done.3 = f32[16,2,512]{2,1,0:T(2,128)S(1)} async-done(((f32[16,2,512]{2,1,0:T(2,128)}), f32[16,2,512]{2,1,0:T(2,128)S(1)}, u32[]{:S(2)}, u32[]{:S(2)}) %all-to-all-start.3) | async-done | bytes 65568 | tf_op jit(solution)/shard_map/all_to_all | solution.py:162
  568.7 7.4 %all-to-all-start.4 = ((f32[16,2,512]{2,1,0:T(2,128)}), f32[16,2,512]{2,1,0:T(2,128)S(1)}, u32[]{:S(2)}, u32[]{:S(2)}) async-start(f32[16,2,512]{2,1,0:T(2,128)} %reshape.206), calls=%async_computation.4 | async-start | bytes 131072 | tf_op jit(solution)/shard_map/all_to_all | solution.py:169
  (220 shorter events, 304.8 us)
Async XLA Ops:
  3.1 20.5 %collective-permute-start = (bf16[2,3,128,512]{3,2,1,0:T(8,128)(2,1)}, bf16[2,3,128,512]{3,2,1,0:T(8,128)(2,1)}, u32[]{:S(2)}, u32[]{:S(2)}) collective-permute-start(bf16[2,3,128,512]{3,2,1,0:T(8,128)(2,1)} %get-tuple-element.158), channel_id=1, source_target_pairs={{3,0},{4,1},{5,2},{6,3},{7,4},{8,5},{9,6},{10,7},{11,8},{12,9},{13... | collective-permute-start | bytes 2359304 | tf_op jit(solution)/shard_map/ppermute | solution.py:22
  4.4 23.7 %collective-permute-start.1 = (bf16[2,3,128,512]{3,2,1,0:T(8,128)(2,1)}, bf16[2,3,128,512]{3,2,1,0:T(8,128)(2,1)S(1)}, u32[]{:S(2)}, u32[]{:S(2)}) collective-permute-start(bf16[2,3,128,512]{3,2,1,0:T(8,128)(2,1)} %get-tuple-element.158), channel_id=1, source_target_pairs={{2,0},{3,1},{4,2},{5,3},{6,4},{7,5},{8,6},{9,7},{10,8},{11,9},{12,... | collective-permute-start | bytes 2359304 | tf_op jit(solution)/shard_map/ppermute | solution.py:22
  5.7 23.4 %collective-permute-start.2 = (bf16[2,3,128,512]{3,2,1,0:T(8,128)(2,1)}, bf16[2,3,128,512]{3,2,1,0:T(8,128)(2,1)S(1)}, u32[]{:S(2)}, u32[]{:S(2)}) collective-permute-start(bf16[2,3,128,512]{3,2,1,0:T(8,128)(2,1)} %get-tuple-element.158), channel_id=1, source_target_pairs={{1,0},{2,1},{3,2},{4,3},{5,4},{6,5},{7,6},{8,7},{9,8},{10,9},{11,1... | collective-permute-start | bytes 2359304 | tf_op jit(solution)/shard_map/ppermute | solution.py:22
  7.0 23.0 %collective-permute-start.3 = (bf16[2,3,128,512]{3,2,1,0:T(8,128)(2,1)}, bf16[2,3,128,512]{3,2,1,0:T(8,128)(2,1)S(1)}, u32[]{:S(2)}, u32[]{:S(2)}) collective-permute-start(bf16[2,3,128,512]{3,2,1,0:T(8,128)(2,1)} %get-tuple-element.158), channel_id=1, source_target_pairs={{0,1},{1,2},{2,3},{3,4},{4,5},{5,6},{6,7},{7,8},{8,9},{9,10},{10,1... | collective-permute-start | bytes 2359304 | tf_op jit(solution)/shard_map/ppermute | solution.py:22
  10.1 53.8 %collective-permute-start.4 = (bf16[2,3,128,512]{3,2,1,0:T(8,128)(2,1)}, bf16[2,3,128,512]{3,2,1,0:T(8,128)(2,1)S(1)}, u32[]{:S(2)}, u32[]{:S(2)}) collective-permute-start(bf16[2,3,128,512]{3,2,1,0:T(8,128)(2,1)} %get-tuple-element.158), channel_id=1, source_target_pairs={{0,2},{1,3},{2,4},{3,5},{4,6},{5,7},{6,8},{7,9},{8,10},{9,11},{10,... | collective-permute-start | bytes 2359304 | tf_op jit(solution)/shard_map/ppermute | solution.py:22
  23.6 55.6 %collective-permute-start.5 = (bf16[2,3,128,512]{3,2,1,0:T(8,128)(2,1)}, bf16[2,3,128,512]{3,2,1,0:T(8,128)(2,1)}, u32[]{:S(2)}, u32[]{:S(2)}) collective-permute-start(bf16[2,3,128,512]{3,2,1,0:T(8,128)(2,1)} %get-tuple-element.158), channel_id=1, source_target_pairs={{0,3},{1,4},{2,5},{3,6},{4,7},{5,8},{6,9},{7,10},{8,11},{9,12},{10... | collective-permute-start | bytes 2359304 | tf_op jit(solution)/shard_map/ppermute | solution.py:22
  399.0 8.9 %copy-start.9 = (s32[16]{0:T(128)S(1)}, s32[16]{0:T(128)}, u32[]{:S(2)}) copy-start(s32[16]{0:T(128)} %param.22) | copy-start | bytes 196
  399.0 25.0 %copy-start.4 = (bf16[128,512]{1,0:T(8,128)(2,1)S(1)}, bf16[128,512]{1,0:T(8,128)(2,1)}, u32[]{:S(2)}) copy-start(bf16[128,512]{1,0:T(8,128)(2,1)} %param.25) | copy-start | bytes 393220
  399.0 25.8 %copy-start.5 = (bf16[128,512]{1,0:T(8,128)(2,1)S(1)}, bf16[128,512]{1,0:T(8,128)(2,1)}, u32[]{:S(2)}) copy-start(bf16[128,512]{1,0:T(8,128)(2,1)} %param.24) | copy-start | bytes 393220
  399.0 27.3 %copy-start.6 = (bf16[128,512]{1,0:T(8,128)(2,1)S(1)}, bf16[128,512]{1,0:T(8,128)(2,1)}, u32[]{:S(2)}) copy-start(bf16[128,512]{1,0:T(8,128)(2,1)} %param.26) | copy-start | bytes 393220
  406.4 70.9 %collective-permute-start.10 = (f32[2,3,128,512]{3,2,1,0:T(8,128)}, f32[2,3,128,512]{3,2,1,0:T(8,128)S(1)}, u32[]{:S(2)}, u32[]{:S(2)}) collective-permute-start(f32[2,3,128,512]{3,2,1,0:T(8,128)} %get-tuple-element.152), channel_id=1, source_target_pairs={{2,0},{3,1},{4,2},{5,3},{6,4},{7,5},{8,6},{9,7},{10,8},{11,9},{12,... | collective-permute-start | bytes 4718600 | tf_op jit(solution)/shard_map/ppermute | solution.py:22
  409.3 39.2 %all-to-all-start = ((bf16[16,1,2]{2,1,0:T(2,128)(2,1)}), bf16[16,1,2]{2,1,0:T(2,128)(2,1)S(1)}, u32[]{:S(2)}, u32[]{:S(2)}) async-start(bf16[16,1,2]{2,1,0:T(2,128)(2,1)} %all_to_all.24), calls=%async_computation | async-start | bytes 16384 | tf_op jit(solution)/shard_map/all_to_all | solution.py:154
  424.9 58.4 %copy-start.1 = (bf16[128,512]{0,1:T(8,128)(2,1)}, bf16[128,512]{0,1:T(8,128)(2,1)S(1)}, u32[]{:S(2)}) copy-start(bf16[128,512]{0,1:T(8,128)(2,1)S(1)} %copy.100) | copy-start | bytes 393220
  448.4 10.1 %all-to-all-start.1 = ((bf16[16,2,512]{2,1,0:T(2,128)(2,1)}), bf16[16,2,512]{2,1,0:T(2,128)(2,1)S(1)}, u32[]{:S(2)}, u32[]{:S(2)}) async-start(bf16[16,2,512]{2,1,0:T(2,128)(2,1)} %reshape.200), calls=%async_computation.1 | async-start | bytes 65536 | tf_op jit(solution)/shard_map/all_to_all | solution.py:152
  458.5 22.3 %all-to-all-start.2 = ((bf16[16,2,512]{2,1,0:T(2,128)(2,1)}), bf16[16,2,512]{2,1,0:T(2,128)(2,1)S(1)}, u32[]{:S(2)}, u32[]{:S(2)}) async-start(bf16[16,2,512]{2,1,0:T(2,128)(2,1)} %reshape.202), calls=%async_computation.2 | async-start | bytes 65536 | tf_op jit(solution)/shard_map/all_to_all | solution.py:153
  462.3 21.0 %copy-start.3 = (bf16[32,8,64]{0,2,1:T(8,128)(2,1)}, bf16[32,8,64]{0,2,1:T(8,128)(2,1)S(1)}, u32[]{:S(2)}) copy-start(bf16[32,8,64]{0,2,1:T(8,128)(2,1)S(1)} %copy.99) | copy-start | bytes 98308
  462.3 120.7 %collective-permute-start.11 = (f32[2,3,128,512]{3,2,1,0:T(8,128)}, f32[2,3,128,512]{3,2,1,0:T(8,128)}, u32[]{:S(2)}, u32[]{:S(2)}) collective-permute-start(f32[2,3,128,512]{3,2,1,0:T(8,128)} %get-tuple-element.151), channel_id=1, source_target_pairs={{3,0},{4,1},{5,2},{6,3},{7,4},{8,5},{9,6},{10,7},{11,8},{12,9},{13... | collective-permute-start | bytes 4718600 | tf_op jit(solution)/shard_map/ppermute | solution.py:22
  463.6 119.4 %collective-permute-start.6 = (f32[2,3,128,512]{3,2,1,0:T(8,128)}, f32[2,3,128,512]{3,2,1,0:T(8,128)}, u32[]{:S(2)}, u32[]{:S(2)}) collective-permute-start(f32[2,3,128,512]{3,2,1,0:T(8,128)} %get-tuple-element.150), channel_id=1, source_target_pairs={{0,3},{1,4},{2,5},{3,6},{4,7},{5,8},{6,9},{7,10},{8,11},{9,12},{10... | collective-permute-start | bytes 4718600 | tf_op jit(solution)/shard_map/ppermute | solution.py:22
  469.1 114.0 %collective-permute-start.7 = (f32[2,3,128,512]{3,2,1,0:T(8,128)}, f32[2,3,128,512]{3,2,1,0:T(8,128)}, u32[]{:S(2)}, u32[]{:S(2)}) collective-permute-start(f32[2,3,128,512]{3,2,1,0:T(8,128)} %get-tuple-element.155), channel_id=1, source_target_pairs={{0,2},{1,3},{2,4},{3,5},{4,6},{5,7},{6,8},{7,9},{8,10},{9,11},{10,... | collective-permute-start | bytes 4718600 | tf_op jit(solution)/shard_map/ppermute | solution.py:22
  474.9 108.2 %collective-permute-start.8 = (f32[2,3,128,512]{3,2,1,0:T(8,128)}, f32[2,3,128,512]{3,2,1,0:T(8,128)}, u32[]{:S(2)}, u32[]{:S(2)}) collective-permute-start(f32[2,3,128,512]{3,2,1,0:T(8,128)} %get-tuple-element.154), channel_id=1, source_target_pairs={{0,1},{1,2},{2,3},{3,4},{4,5},{5,6},{6,7},{7,8},{8,9},{9,10},{10,1... | collective-permute-start | bytes 4718600 | tf_op jit(solution)/shard_map/ppermute | solution.py:22
  477.3 105.8 %collective-permute-start.9 = (f32[2,3,128,512]{3,2,1,0:T(8,128)S(1)}, f32[2,3,128,512]{3,2,1,0:T(8,128)}, u32[]{:S(2)}, u32[]{:S(2)}) collective-permute-start(f32[2,3,128,512]{3,2,1,0:T(8,128)S(1)} %get-tuple-element.153), channel_id=1, source_target_pairs={{1,0},{2,1},{3,2},{4,3},{5,4},{6,5},{7,6},{8,7},{9,8},{10,9},{11,1... | collective-permute-start | bytes 4718600 | tf_op jit(solution)/shard_map/ppermute | solution.py:22
  496.4 72.3 %all-to-all-start.3 = ((f32[16,2,512]{2,1,0:T(2,128)}), f32[16,2,512]{2,1,0:T(2,128)S(1)}, u32[]{:S(2)}, u32[]{:S(2)}) async-start(f32[16,2,512]{2,1,0:T(2,128)} %reshape.204), calls=%async_computation.3 | async-start | bytes 131072 | tf_op jit(solution)/shard_map/all_to_all | solution.py:162
  507.0 71.6 %copy-start.2 = (bf16[128,8,64]{0,2,1:T(8,128)(2,1)S(1)}, bf16[128,8,64]{0,2,1:T(8,128)(2,1)}, u32[]{:S(2)}) copy-start(bf16[128,8,64]{0,2,1:T(8,128)(2,1)} %slice.95) | copy-start | bytes 393220
  568.7 14.3 %all-to-all-start.4 = ((f32[16,2,512]{2,1,0:T(2,128)}), f32[16,2,512]{2,1,0:T(2,128)S(1)}, u32[]{:S(2)}, u32[]{:S(2)}) async-start(f32[16,2,512]{2,1,0:T(2,128)} %reshape.206), calls=%async_computation.4 | async-start | bytes 131072 | tf_op jit(solution)/shard_map/all_to_all | solution.py:169
  (11 other events, 52.4 us)
where the time goes:
time: 595 us; the launch traced here: 592 us
  local copies, waits for them, and re-layouts  194 us (33%)
  waiting for transfers between devices  141 us (24%)
  other arithmetic  109 us (18%)
  matrix products  85.4 us (14%)
  starting transfers between devices  60.8 us (10%)
    all_to_all x1, waiting for transfers between devices, local(): lax.all_to_all(melt_gk[melt_rows:].reshape(devices, ICAP, width), 'space'...  58.3 us
    ppermute x12, waiting for transfers between devices, shifted_2(): lax.ppermute(value, axis, [(source, source + steps) for source in range(i...  54 us
    scatter-add x3, other arithmetic, gas_block(): grad_slots = grad_slots.at[:, slot_row].add(grad_pair)  53.7 us
    ppermute x12, starting transfers between devices, shifted_2(): lax.ppermute(value, axis, [(source, source + steps) for source in range(i...  32.2 us
    while x24, local copies, waits for them, and re-layouts  26 us
    select_n x3, other arithmetic, gas_block(): grad_pair = jnp.where(entry_ok[None, :, None, None], grad_pair, 0.0)  25.4 us
    all_to_all x1, waiting for transfers between devices, local(): lax.all_to_all(row_flag, 'space', split_axis=0, concat_axis=0, tiled=True)  19 us
    dot_general x4, matrix products, attend(): jnp.einsum('hrs,shd->rhd', weights_low, value_heads, preferred_element_ty...  18.9 us
  transfers between devices with their start and end apart: 17, of which 7 were waited for; matrix products, arithmetic and copies ran while one was open for 8% of the time, Pallas kernels for 0%

commit v1 on v0

v1 whole, which is shorter than its diff:
```python
import functools

import jax
import jax.numpy as jnp
from jax import lax
from jax.experimental import pallas as pl
from jax.experimental.pallas import tpu as pltpu
from jax.sharding import PartitionSpec as P

BLK = 128
LANE = 128
HALF = 64
WIN = 3
ICAP = 2
GB = 3
OFFS = (1, -1, 2, -2, 3, -3)
NOFF = len(OFFS)
CHUNK = 256
PACK = 16
MARK = 1e30
DEAD = 1e30
MESH = pl.DeviceIdType.MESH
F32 = jnp.float32
BF16 = jnp.bfloat16


def iota(shape, dim):
    return lax.broadcasted_iota(jnp.int32, shape, dim)


def onehot(mask):
    return jnp.where(mask, 1.0, 0.0).astype(BF16)


def dot(a, b):
    return jnp.dot(a, b, preferred_element_type=F32)


def dot_nt(a, b):
    return lax.dot_general(a, b, (((1,), (1,)), ((), ())), preferred_element_type=F32)


def any_of(mask):
    hit = jnp.max(jnp.where(mask, 1.0, 0.0), axis=0, keepdims=True)
    return jnp.max(hit, axis=1, keepdims=True)


def split_heads(x, scale):
    lane = iota(x.shape, 1)
    wide = x.astype(F32) * scale
    first = jnp.where(lane < HALF, wide, 0.0).astype(BF16)
    second = jnp.where(lane < HALF, 0.0, wide).astype(BF16)
    return first, second


def kernel(
    n,
    q_ref, k_ref, v_ref, c_ref, ids_ref, val_ref, row_ref, dst_ref, mq_ref, mk_ref, mv_ref, mc_ref,
    o_ref, dq_ref, dk_ref, dv_ref, mo_ref, mdq_ref, mdk_ref, mdv_ref,
    kv, q2, c2, kt, vt, acc, o2, dq2, bias, gsend, gback, grecv, own,
    ipk, irecv, iback, ibrecv, mkv, mbias, iacc,
    gs_sem, gr_sem, bs_sem, br_sem, is_sem, ir_sem, js_sem, jr_sem,
):
    me = lax.axis_index("space")
    rows, width = q_ref.shape
    pairs = width // LANE
    melt = mq_ref.shape[0]
    entries = row_ref.shape[1]
    extra = n * ICAP
    keys = rows + NOFF * BLK

    barrier = pltpu.get_barrier_semaphore()

    @pl.loop(1, n)
    def _(d):
        pl.semaphore_signal(
            barrier, inc=1, device_id={"space": lax.rem(me + d, n)}, device_id_type=MESH
        )

    ids = jnp.where(val_ref[...] == 1, ids_ref[...], -1000)
    block = iota(ids.shape, 0)
    picks = []
    for off in OFFS:
        reader = me + off
        mine = (block >= reader * GB) & (block < reader * GB + GB)
        picks.append([any_of(mine & (ids == me * GB + b)) for b in range(GB)])
    live = []
    for b in range(GB):
        mine = block == me * GB + b
        row = [any_of(mine & (ids == me * GB + s)) for s in range(GB)]
        for off in OFFS:
            owner = me - off
            row.append(any_of(mine & (ids >= owner * GB) & (ids < owner * GB + GB)))
        live.append(row)
    for s in range(GB + NOFF):
        parts = [
            jnp.broadcast_to((1.0 - live[b][s]) * DEAD, (1, BLK)) for b in range(GB)
        ]
        bias[s : s + 1, :] = jnp.concatenate(parts + parts, axis=1)

    for i in range(NOFF):
        for j, ref in enumerate((k_ref, v_ref)):
            picked = sum(
                ref[b * BLK : (b + 1) * BLK, :].astype(F32) * picks[i][b] for b in range(GB)
            ).astype(BF16)
            for p in range(pairs):
                gsend[p, i, j] = picked[:, p * LANE : (p + 1) * LANE]

    e_r, e_c = iota((entries, entries), 0), iota((entries, entries), 1)
    dst_row = dst_ref[...].astype(F32)
    dst_col = jnp.sum(jnp.where(e_r == e_c, dst_row, 0.0), axis=1, keepdims=True)
    row_row = row_ref[...].astype(F32)
    row_col = jnp.sum(jnp.where(e_r == e_c, row_row, 0.0), axis=1, keepdims=True)
    same = dst_row == dst_col
    rank_row = jnp.sum(jnp.where(same & (e_r < e_c), 1.0, 0.0), axis=0, keepdims=True)
    rank_col = jnp.sum(jnp.where(same & (e_c < e_r), 1.0, 0.0), axis=1, keepdims=True)
    place_row = (dst_row * PACK + rank_row).astype(jnp.int32)
    place_col = (dst_col * PACK + rank_col).astype(jnp.int32)
    take = onehot(iota((entries, rows), 1) == row_col.astype(jnp.int32))
    packed = jnp.zeros((n * PACK, LANE), F32)
    count = jnp.zeros((n * PACK, 1), F32)
    slot_iota = iota((n * PACK, entries), 0)
    for j, ref in enumerate((k_ref, v_ref)):
        rows_taken = dot(take, ref[...]).astype(BF16)
        for p in range(pairs):
            hit = slot_iota == place_row + (2 * p + 8 * j)
            packed += dot(onehot(hit), rows_taken[:, p * LANE : (p + 1) * LANE])
            count += jnp.sum(jnp.where(hit, 1.0, 0.0), axis=1, keepdims=True)
    packed = jnp.where(count > 0.5, packed, MARK).astype(BF16)
    ipk[...] = packed.reshape(n, PACK, LANE)

    pl.semaphore_wait(barrier, n - 1)

    def gas_copy(p, i):
        s = rows + i * BLK
        return pltpu.make_async_remote_copy(
            src_ref=gsend.at[p, i],
            dst_ref=kv.at[p, :, pl.ds(s, BLK), :],
            send_sem=gs_sem.at[p, i],
            recv_sem=gr_sem.at[p, i],
            device_id={"space": me + OFFS[i]},
            device_id_type=MESH,
        )

    def back_copy(p, i):
        return pltpu.make_async_remote_copy(
            src_ref=gback.at[p, i],
            dst_ref=grecv.at[p, i],
            send_sem=bs_sem.at[p, i],
            recv_sem=br_sem.at[p, i],
            device_id={"space": me - OFFS[i]},
            device_id_type=MESH,
        )

    def iface_copy(src, dst, ssem, rsem, peer, slot):
        return pltpu.make_async_remote_copy(
            src_ref=src.at[peer],
            dst_ref=dst.at[slot],
            send_sem=ssem.at[peer],
            recv_sem=rsem.at[slot],
            device_id={"space": peer},
            device_id_type=MESH,
        )

    def has(dev):
        return (dev >= 0) & (dev < n)

    def gas_start(p):
        for i, off in enumerate(OFFS):
            @pl.when(has(me + off))
            def _():
                gas_copy(p, i).start()

    gas_start(0)

    @pl.loop(1, n)
    def _(d):
        peer = lax.rem(me + d, n)
        iface_copy(ipk, irecv, is_sem, ir_sem, peer, me).start()

    @pl.loop(1, pairs)
    def _(p):
        gas_start(p)

    irecv[me] = ipk[me]
    for p in range(pairs):
        lanes = slice(p * LANE, (p + 1) * LANE)
        for j, ref in enumerate((k_ref, v_ref)):
            kv[p, j, :rows, :] = ref[:, lanes]
        for j, ref in enumerate((mk_ref, mv_ref)):
            mkv[p, j, :melt, :] = ref[:, lanes]
    for i, off in enumerate(OFFS):
        @pl.when(jnp.logical_not(has(me - off)))
        def _():
            s = rows + i * BLK
            kv[:, :, s : s + BLK, :] = jnp.zeros((pairs, 2, BLK, LANE), BF16)

    def gas_pair(p):
        lanes = pl.ds(pl.multiple_of(p * LANE, LANE), LANE)
        qa, qb = split_heads(q_ref[:, lanes], 0.125)
        q2[:rows, :], q2[rows:, :] = qa, qb
        ca, cb = split_heads(c_ref[:, lanes], 1.0)
        c2[:rows, :], c2[rows:, :] = ca, cb
        for i, off in enumerate(OFFS):
            @pl.when(has(me - off))
            def _():
                gas_copy(p, i).wait_recv()
        kt[...] = kv[p, 0].T
        vt[...] = kv[p, 1].T
        for c in range(2 * rows // CHUNK):
            part = slice(c * CHUNK, (c + 1) * CHUNK)
            qc, cc = q2[part, :], c2[part, :]
            slots = GB + NOFF
            sc = dot_nt(kv[p, 0], qc)
            blk = [sc[s * BLK : (s + 1) * BLK, :] for s in range(slots)]
            pen = [bias[s : s + 1, part] for s in range(slots)]
            top = functools.reduce(
                jnp.maximum,
                [jnp.max(blk[s], axis=0, keepdims=True) - pen[s] for s in range(slots)],
            )
            dp = dot_nt(kv[p, 1], cc)
            ex = [jnp.exp(blk[s] - (top + pen[s])) for s in range(slots)]
            dps = [dp[s * BLK : (s + 1) * BLK, :] for s in range(slots)]
            total = sum(jnp.sum(e, axis=0, keepdims=True) for e in ex)
            inv = 1.0 / total
            delta = inv * sum(
                jnp.sum(e * d, axis=0, keepdims=True) for e, d in zip(ex, dps)
            )
            low, ds = [], []
            for e, d in zip(ex, dps):
                w = e * inv
                low.append(w.astype(BF16))
                ds.append((w * (d - delta)).astype(BF16))
            low = jnp.concatenate(low, axis=0)
            ds = jnp.concatenate(ds, axis=0)
            dv = dot(low, cc)
            dk = dot(ds, qc)
            if c == 0:
                acc[0], acc[1] = dk, dv
            else:
                acc[0] += dk
                acc[1] += dv
            o2[part, :] = dot(vt[...], low).T
            dq2[part, :] = dot(kt[...], ds).T
        lane = iota((rows, LANE), 1)
        o_ref[:, lanes] = jnp.where(lane < HALF, o2[:rows, :], o2[rows:, :]).astype(BF16)
        dq_ref[:, lanes] = (
            jnp.where(lane < HALF, dq2[:rows, :], dq2[rows:, :]) * 0.125
        ).astype(BF16)
        for i, off in enumerate(OFFS):
            s = rows + i * BLK
            gback[p, i] = acc[:, s : s + BLK, :].astype(BF16)

            @pl.when(has(me - off))
            def _():
                back_copy(p, i).start()
        own[p] = acc[:, :rows, :]

    def melt_all():
        @pl.loop(1, n)
        def _(d):
            peer = lax.rem(me + d, n)
            iface_copy(ipk, irecv, is_sem, ir_sem, peer, peer).wait_recv()

        flat = irecv[...].reshape(n * PACK, LANE)
        s_col = iota((extra, n * PACK), 0)
        r_row = iota((extra, n * PACK), 1)
        home = (s_col >> 1) * PACK + (s_col & 1)
        good = None
        for j in range(2):
            for p in range(pairs):
                got = dot(onehot(r_row == home + (2 * p + 8 * j)), flat)
                if good is None:
                    good = jnp.max(got, axis=1, keepdims=True) < 0.1 * MARK
                mkv[p, j, melt:, :] = jnp.where(good, got, 0.0).astype(BF16)
        mbias[:melt, :] = jnp.zeros((melt, LANE), F32)
        mbias[melt:, :] = jnp.broadcast_to(jnp.where(good, 0.0, DEAD), (extra, LANE))
        iacc[...] = jnp.zeros_like(iacc)
        u_row = iota((n * PACK, extra), 0)
        u_col = iota((n * PACK, extra), 1)
        back_home = (u_col >> 1) * PACK + (u_col & 1)

        @pl.loop(0, pairs)
        def _(p):
            lanes = pl.ds(pl.multiple_of(p * LANE, LANE), LANE)
            qc = jnp.concatenate(split_heads(mq_ref[:, lanes], 0.125), axis=0)
            cc = jnp.concatenate(split_heads(mc_ref[:, lanes], 1.0), axis=0)
            kp, vp = mkv[p, 0], mkv[p, 1]
            sc = dot_nt(kp, qc) - mbias[:, :1]
            ex = jnp.exp(sc - jnp.max(sc, axis=0, keepdims=True))
            w = ex * (1.0 / jnp.sum(ex, axis=0, keepdims=True))
            dp = dot_nt(vp, cc)
            delta = jnp.sum(w * dp, axis=0, keepdims=True)
            ds = (w * (dp - delta)).astype(BF16)
            low = w.astype(BF16)
            dv = dot(low, cc)
            dk = dot(ds, qc)
            out = dot(vp.T, low).T
            dq = dot(kp.T, ds).T
            lane = iota((melt, LANE), 1)
            mo_ref[:, lanes] = jnp.where(lane < HALF, out[:melt], out[melt:]).astype(BF16)
            mdq_ref[:, lanes] = (
                jnp.where(lane < HALF, dq[:melt], dq[melt:]) * 0.125
            ).astype(BF16)
            mdk_ref[:, lanes] = dk[:melt].astype(BF16)
            mdv_ref[:, lanes] = dv[:melt].astype(BF16)
            iacc[...] += dot(
                onehot(u_row == back_home + 2 * p), dk[melt:].astype(BF16)
            ) + dot(onehot(u_row == back_home + (2 * p + 8)), dv[melt:].astype(BF16))

        iback[...] = iacc[...].astype(BF16).reshape(n, PACK, LANE)

        @pl.loop(1, n)
        def _(d):
            peer = lax.rem(me + d, n)
            iface_copy(iback, ibrecv, js_sem, jr_sem, peer, me).start()

        ibrecv[me] = iback[me]

    gas_pair(0)
    melt_all()

    @pl.loop(1, pairs)
    def _(p):
        gas_pair(p)

    @pl.loop(0, pairs)
    def _(p):
        for i, off in enumerate(OFFS):
            @pl.when(has(me + off))
            def _():
                back_copy(p, i).wait_recv()
                got = grecv[p, i].astype(F32)
                for b in range(GB):
                    own[p, :, b * BLK : (b + 1) * BLK, :] += got * picks[i][b]

    @pl.loop(1, n)
    def _(d):
        peer = lax.rem(me + d, n)
        iface_copy(iback, ibrecv, js_sem, jr_sem, peer, peer).wait_recv()

    flat = ibrecv[...].reshape(n * PACK, LANE)
    put = onehot(iota((rows, entries), 0) == row_row.astype(jnp.int32))
    slot_lane = iota((entries, n * PACK), 1)
    for j, ref in enumerate((dk_ref, dv_ref)):
        for p in range(pairs):
            mine = dot(onehot(slot_lane == place_col + (2 * p + 8 * j)), flat).astype(BF16)
            ref[:, p * LANE : (p + 1) * LANE] = (own[p, j] + dot(put, mine)).astype(BF16)

    @pl.loop(0, pairs)
    def _(p):
        for i, off in enumerate(OFFS):
            @pl.when(has(me + off))
            def _():
                gas_copy(p, i).wait_send()

            @pl.when(has(me - off))
            def _():
                back_copy(p, i).wait_send()

    @pl.loop(1, n)
    def _(d):
        peer = lax.rem(me + d, n)
        iface_copy(ipk, irecv, is_sem, ir_sem, peer, me).wait_send()
        iface_copy(iback, ibrecv, js_sem, jr_sem, peer, me).wait_send()


def local(n, *args):
    q, k, v, c, ids, val, if_row, if_dst, mq, mk, mv, mc = args
    rows, width = q.shape
    melt = mq.shape[0]
    pairs = width // LANE
    keys = rows + NOFF * BLK
    extra = n * ICAP
    dma = pltpu.SemaphoreType.DMA
    vmem = pl.BlockSpec(memory_space=pltpu.VMEM)
    gas_out = jax.ShapeDtypeStruct((rows, width), BF16)
    melt_out = jax.ShapeDtypeStruct((melt, width), BF16)
    heads = width // HALF
    pieces = heads * (rows * keys + melt * (melt + extra))
    return pl.pallas_call(
        functools.partial(kernel, n),
        out_shape=[gas_out] * 4 + [melt_out] * 4,
        in_specs=[vmem] * 12,
        out_specs=[vmem] * 8,
        scratch_shapes=[
            pltpu.VMEM((pairs, 2, keys, LANE), BF16),
            pltpu.VMEM((2 * rows, LANE), BF16),
            pltpu.VMEM((2 * rows, LANE), BF16),
            pltpu.VMEM((LANE, keys), BF16),
            pltpu.VMEM((LANE, keys), BF16),
            pltpu.VMEM((2, keys, LANE), F32),
            pltpu.VMEM((2 * rows, LANE), F32),
            pltpu.VMEM((2 * rows, LANE), F32),
            pltpu.VMEM((16, 2 * rows), F32),
            pltpu.VMEM((pairs, NOFF, 2, BLK, LANE), BF16),
            pltpu.VMEM((pairs, NOFF, 2, BLK, LANE), BF16),
            pltpu.VMEM((pairs, NOFF, 2, BLK, LANE), BF16),
            pltpu.VMEM((pairs, 2, rows, LANE), F32),
            pltpu.VMEM((n, PACK, LANE), BF16),
            pltpu.VMEM((n, PACK, LANE), BF16),
            pltpu.VMEM((n, PACK, LANE), BF16),
            pltpu.VMEM((n, PACK, LANE), BF16),
            pltpu.VMEM((pairs, 2, melt + extra, LANE), BF16),
            pltpu.VMEM((melt + extra, LANE), F32),
            pltpu.VMEM((n * PACK, LANE), F32),
            dma((pairs, NOFF)),
            dma((pairs, NOFF)),
            dma((pairs, NOFF)),
            dma((pairs, NOFF)),
            dma((n,)),
            dma((n,)),
            dma((n,)),
            dma((n,)),
        ],
        compiler_params=pltpu.CompilerParams(
            collective_id=0, has_side_effects=True, vmem_limit_bytes=48 * 2**20
        ),
        cost_estimate=pl.CostEstimate(
            flops=pieces * HALF * 10,
            bytes_accessed=16 * width * (rows + melt),
            transcendentals=pieces,
        ),
    )(q, k, v, c, ids, val, if_row.reshape(1, -1), if_dst.reshape(1, -1), mq, mk, mv, mc)


def solution(mesh):
    both = P(("parts", "space"), None)
    flat = P(("parts", "space"))
    listed = P("parts", None)
    return jax.shard_map(
        functools.partial(local, mesh.shape["space"]),
        mesh=mesh,
        in_specs=(both, both, both, both, listed, listed, flat, flat, both, both, both, both),
        out_specs=(both,) * 8,
        check_vma=False,
    )
```

time: 595 us -> 70.9 us (0.12)
  local copies, waits for them, and re-layouts: 194 us -> 14.6 us
  waiting for transfers between devices: 141 us -> 0 us
  other arithmetic: 109 us -> 0 us
  matrix products: 85.4 us -> 0 us
  starting transfers between devices: 60.8 us -> 0 us
  Pallas kernels: 0 us -> 54.5 us
    all_to_all x5 -> x0, waiting for transfers between devices: 87.4 us -> none  [the longest x1 58.3 us: local(): lax.all_to_all(melt_gk[melt_rows:].reshape(devices, ICAP, width), 'space'...]
    dot_general x20 -> x0, matrix products: 68.9 us -> none  [the longest x4 18.9 us: attend(): jnp.einsum('hrs,shd->rhd', weights_low, value_heads, preferred_element_ty...]
    scatter-add x5 -> x0, other arithmetic: 55.8 us -> none  [the longest x3 53.7 us: gas_block(): grad_slots = grad_slots.at[:, slot_row].add(grad_pair)]
    pallas_call x0 -> x1, Pallas kernels: none -> 54.5 us  [local(): pl.pallas_call(functools.partial(kernel, n), out_shape=[gas_out] * 4 + [m...]
    ppermute x12 -> x0, waiting for transfers between devices: 54 us -> none  [shifted_2(): lax.ppermute(value, axis, [(source, source + steps) for source in range(i...]
    reshape x15 -> x0, local copies, waits for them, and re-layouts: 43 us -> none  [the longest x3 15.8 us: gas_block(): jnp.stack([grad_key.reshape(list_len, BLK, width), grad_value.reshape(lis...]
    select_n x13 -> x0, other arithmetic: 37.6 us -> none  [the longest x3 25.4 us: gas_block(): grad_pair = jnp.where(entry_ok[None, :, None, None], grad_pair, 0.0)]
    ppermute x12 -> x0, starting transfers between devices: 32.2 us -> none  [shifted_2(): lax.ppermute(value, axis, [(source, source + steps) for source in range(i...]
  transfers between devices with their start and end apart: 17 -> 0, of which waited for: 7 -> 0; matrix products, arithmetic and copies ran while one was open for 8% -> 0% of each run, Pallas kernels for 0% -> 0%
where the time goes in v1:
time: 70.9 us; the launch traced here: 69.8 us
  Pallas kernels  54.5 us (77%)
  local copies, waits for them, and re-layouts  14.6 us (21%)
    pallas_call x1, Pallas kernels, local(): pl.pallas_call(functools.partial(kernel, n), out_shape=[gas_out] * 4 + [m...  54.5 us
    unnamed x32, local copies, waits for them, and re-layouts  14.6 us

profile of v1, /device:TPU:0, one launch (start us, length us, event | category | flops | bytes accessed | tf_op | source)
XLA Modules:
  0.0 69.8 jit_solution(18175228339013166223)
XLA Ops:
  0.6 0.0 copy-start.10
  0.6 0.8 %copy.20.ids_ref = s32[48,16]{1,0:T(8,128)S(1)} copy(s32[48,16]{0,1:T(8,128)} %param.16) | data formatting | bytes 6144 | tf_op args[4]
  1.4 0.0 copy-done.10
  1.4 0.0 copy-start.9
  1.4 0.1 copy.21.val_ref
  1.5 0.6 copy-done.8
  2.1 0.0 copy-done.9
  2.1 1.0 %copy-done = bf16[384,512]{1,0:T(8,128)(2,1)S(1)} copy-done((bf16[384,512]{1,0:T(8,128)(2,1)S(1)}, bf16[384,512]{1,0:T(8,128)(2,1)}, u32[]{:S(2)}) %copy-start) | copy-done | bytes 393240
  3.1 1.0 %copy-done.1 = bf16[384,512]{1,0:T(8,128)(2,1)S(1)} copy-done((bf16[384,512]{1,0:T(8,128)(2,1)S(1)}, bf16[384,512]{1,0:T(8,128)(2,1)}, u32[]{:S(2)}) %copy-start.1) | copy-done | bytes 393240
  4.1 1.0 %copy-done.2 = bf16[384,512]{1,0:T(8,128)(2,1)S(1)} copy-done((bf16[384,512]{1,0:T(8,128)(2,1)S(1)}, bf16[384,512]{1,0:T(8,128)(2,1)}, u32[]{:S(2)}) %copy-start.2) | copy-done | bytes 393240
  5.1 1.0 %copy-done.3 = bf16[384,512]{1,0:T(8,128)(2,1)S(1)} copy-done((bf16[384,512]{1,0:T(8,128)(2,1)S(1)}, bf16[384,512]{1,0:T(8,128)(2,1)}, u32[]{:S(2)}) %copy-start.3) | copy-done | bytes 393240
  6.1 0.9 %copy-done.4 = bf16[128,512]{1,0:T(8,128)(2,1)S(1)} copy-done((bf16[128,512]{1,0:T(8,128)(2,1)S(1)}, bf16[128,512]{1,0:T(8,128)(2,1)}, u32[]{:S(2)}) %copy-start.4) | copy-done | bytes 131096
  7.0 0.9 %copy-done.5 = bf16[128,512]{1,0:T(8,128)(2,1)S(1)} copy-done((bf16[128,512]{1,0:T(8,128)(2,1)S(1)}, bf16[128,512]{1,0:T(8,128)(2,1)}, u32[]{:S(2)}) %copy-start.5) | copy-done | bytes 131096
  7.9 0.9 %copy-done.6 = bf16[128,512]{1,0:T(8,128)(2,1)S(1)} copy-done((bf16[128,512]{1,0:T(8,128)(2,1)S(1)}, bf16[128,512]{1,0:T(8,128)(2,1)}, u32[]{:S(2)}) %copy-start.6) | copy-done | bytes 131096
  8.8 0.9 %copy-done.7 = bf16[128,512]{1,0:T(8,128)(2,1)S(1)} copy-done((bf16[128,512]{1,0:T(8,128)(2,1)S(1)}, bf16[128,512]{1,0:T(8,128)(2,1)}, u32[]{:S(2)}) %copy-start.7) | copy-done | bytes 131096
  9.7 54.5 %shard_map.179 = (bf16[384,512]{1,0:T(8,128)(2,1)S(1)}, bf16[384,512]{1,0:T(8,128)(2,1)S(1)}, bf16[384,512]{1,0:T(8,128)(2,1)S(1)}, bf16[384,512]{1,0:T(8,128)(2...) custom-call(bf16[384,512]{1,0:T(8,128)(2,1)S(1)} %copy-done, ...), custom_call_target="tpu_custom_call" | custom-call | flops 2369781760 | bytes 4194304 | tf_op jit(solution)/shard_map/pallas_call | solution.py:381
  64.2 0.7 %copy.30 = bf16[384,512]{1,0:T(8,128)(2,1)} copy(bf16[384,512]{1,0:T(8,128)(2,1)S(1)} %get-tuple-element.16) | data formatting | bytes 786432
  64.9 0.7 %copy.31 = bf16[384,512]{1,0:T(8,128)(2,1)} copy(bf16[384,512]{1,0:T(8,128)(2,1)S(1)} %get-tuple-element.17) | data formatting | bytes 786432
  65.7 0.7 %copy.32 = bf16[384,512]{1,0:T(8,128)(2,1)} copy(bf16[384,512]{1,0:T(8,128)(2,1)S(1)} %get-tuple-element.18) | data formatting | bytes 786432
  66.4 0.7 %copy.33 = bf16[384,512]{1,0:T(8,128)(2,1)} copy(bf16[384,512]{1,0:T(8,128)(2,1)S(1)} %get-tuple-element.19) | data formatting | bytes 786432
  67.2 0.7 copy.34
  67.8 0.7 copy.35
  68.5 0.7 copy.36
  69.1 0.7 copy.37
  (9 shorter events, 0.0 us)
Async XLA Ops:
  0.6 0.8 %copy-start.10 = (s32[48,16]{0,1:T(8,128)S(1)}, s32[48,16]{0,1:T(8,128)}, u32[]{:S(2)}) copy-start(s32[48,16]{0,1:T(8,128)} %param.17) | copy-start | bytes 9220
  1.4 0.7 copy-start.8
  1.4 0.7 copy-start.9
  2.1 1.0 %copy-start = (bf16[384,512]{1,0:T(8,128)(2,1)S(1)}, bf16[384,512]{1,0:T(8,128)(2,1)}, u32[]{:S(2)}) copy-start(bf16[384,512]{1,0:T(8,128)(2,1)} %q_ref.1) | copy-start | bytes 1179652
  3.1 1.0 %copy-start.1 = (bf16[384,512]{1,0:T(8,128)(2,1)S(1)}, bf16[384,512]{1,0:T(8,128)(2,1)}, u32[]{:S(2)}) copy-start(bf16[384,512]{1,0:T(8,128)(2,1)} %k_ref.1) | copy-start | bytes 1179652
  4.1 1.0 %copy-start.2 = (bf16[384,512]{1,0:T(8,128)(2,1)S(1)}, bf16[384,512]{1,0:T(8,128)(2,1)}, u32[]{:S(2)}) copy-start(bf16[384,512]{1,0:T(8,128)(2,1)} %v_ref.1) | copy-start | bytes 1179652
  5.1 1.0 %copy-start.3 = (bf16[384,512]{1,0:T(8,128)(2,1)S(1)}, bf16[384,512]{1,0:T(8,128)(2,1)}, u32[]{:S(2)}) copy-start(bf16[384,512]{1,0:T(8,128)(2,1)} %c_ref.1) | copy-start | bytes 1179652
  6.1 0.9 %copy-start.4 = (bf16[128,512]{1,0:T(8,128)(2,1)S(1)}, bf16[128,512]{1,0:T(8,128)(2,1)}, u32[]{:S(2)}) copy-start(bf16[128,512]{1,0:T(8,128)(2,1)} %mq_ref.1) | copy-start | bytes 393220
  7.0 0.9 %copy-start.5 = (bf16[128,512]{1,0:T(8,128)(2,1)S(1)}, bf16[128,512]{1,0:T(8,128)(2,1)}, u32[]{:S(2)}) copy-start(bf16[128,512]{1,0:T(8,128)(2,1)} %mk_ref.1) | copy-start | bytes 393220
  7.9 0.9 %copy-start.6 = (bf16[128,512]{1,0:T(8,128)(2,1)S(1)}, bf16[128,512]{1,0:T(8,128)(2,1)}, u32[]{:S(2)}) copy-start(bf16[128,512]{1,0:T(8,128)(2,1)} %mv_ref.1) | copy-start | bytes 393220
  8.8 0.9 %copy-start.7 = (bf16[128,512]{1,0:T(8,128)(2,1)S(1)}, bf16[128,512]{1,0:T(8,128)(2,1)}, u32[]{:S(2)}) copy-start(bf16[128,512]{1,0:T(8,128)(2,1)} %mc_ref.1) | copy-start | bytes 393220

commit v2 on v1

--- a/solution.py
+++ b/solution.py
@@ -55,13 +55,26 @@
 
 def kernel(
     n,
+    q_hbm, k_hbm, v_hbm, c_hbm, ids_hbm, val_hbm, row_hbm, dst_hbm, mq_hbm, mk_hbm, mv_hbm, mc_hbm,
+    o_ref, dq_ref, dk_ref, dv_ref, mo_ref, mdq_ref, mdk_ref, mdv_ref,
     q_ref, k_ref, v_ref, c_ref, ids_ref, val_ref, row_ref, dst_ref, mq_ref, mk_ref, mv_ref, mc_ref,
-    o_ref, dq_ref, dk_ref, dv_ref, mo_ref, mdq_ref, mdk_ref, mdv_ref,
-    kv, q2, c2, kt, vt, acc, o2, dq2, bias, gsend, gback, grecv, own,
+    in_sem, kv, q2, c2, kt, vt, acc, o2, dq2, bias, gsend, gback, grecv, own,
     ipk, irecv, iback, ibrecv, mkv, mbias, iacc,
     gs_sem, gr_sem, bs_sem, br_sem, is_sem, ir_sem, js_sem, jr_sem,
 ):
     me = lax.axis_index("space")
+    loads = [
+        pltpu.make_async_copy(src, dst, in_sem.at[i])
+        for i, (src, dst) in enumerate(
+            (
+                (ids_hbm, ids_ref), (val_hbm, val_ref), (k_hbm, k_ref), (v_hbm, v_ref),
+                (row_hbm, row_ref), (dst_hbm, dst_ref), (mk_hbm, mk_ref), (mv_hbm, mv_ref),
+                (q_hbm, q_ref), (c_hbm, c_ref), (mq_hbm, mq_ref), (mc_hbm, mc_ref),
+            )
+        )
+    ]
+    for load in loads:
+        load.start()
     rows, width = q_ref.shape
     pairs = width // LANE
     melt = mq_ref.shape[0]
@@ -77,13 +90,106 @@
             barrier, inc=1, device_id={"space": lax.rem(me + d, n)}, device_id_type=MESH
         )
 
+    for load in loads[:2]:
+        load.wait()
+
     ids = jnp.where(val_ref[...] == 1, ids_ref[...], -1000)
-    block = iota(ids.shape, 0)
+    block = iota(ids.shape, 1)
     picks = []
     for off in OFFS:
         reader = me + off
         mine = (block >= reader * GB) & (block < reader * GB + GB)
         picks.append([any_of(mine & (ids == me * GB + b)) for b in range(GB)])
+    def gas_copy(p, i):
+        s = rows + i * BLK
+        return pltpu.make_async_remote_copy(
+            src_ref=gsend.at[p, i],
+            dst_ref=kv.at[p, :, pl.ds(s, BLK), :],
+            send_sem=gs_sem.at[p, i],
+            recv_sem=gr_sem.at[p, i],
+            device_id={"space": me + OFFS[i]},
+            device_id_type=MESH,
+        )
+
+    def back_copy(p, i):
+        return pltpu.make_async_remote_copy(
+            src_ref=gback.at[p, i],
+            dst_ref=grecv.at[p, i],
+            send_sem=bs_sem.at[p, i],
+            recv_sem=br_sem.at[p, i],
+            device_id={"space": me - OFFS[i]},
+            device_id_type=MESH,
+        )
+
+    def iface_copy(src, dst, ssem, rsem, peer, slot):
+        return pltpu.make_async_remote_copy(
+            src_ref=src.at[peer],
+            dst_ref=dst.at[slot],
+            send_sem=ssem.at[peer],
+            recv_sem=rsem.at[slot],
+            device_id={"space": peer},
+            device_id_type=MESH,
+        )
+
+    def has(dev):
+        return (dev >= 0) & (dev < n)
+
+    def gas_start(p):
+        lanes = pl.ds(pl.multiple_of(p * LANE, LANE), LANE)
+        for i, off in enumerate(OFFS):
+            for j, ref in enumerate((k_ref, v_ref)):
+                gsend[p, i, j] = sum(
+                    ref[b * BLK : (b + 1) * BLK, lanes].astype(F32) * picks[i][b]
+                    for b in range(GB)
+                ).astype(BF16)
+
+            @pl.when(has(me + off))
+            def _():
+                gas_copy(p, i).start()
+
+    for load in loads[2:4]:
+        load.wait()
+    pl.semaphore_wait(barrier, n - 1)
+
+    @pl.loop(0, 2)
+    def _(p):
+        gas_start(p)
+
+    for load in loads[4:6]:
+        load.wait()
+    e_r, e_c = iota((entries, entries), 0), iota((entries, entries), 1)
+    dst_row = dst_ref[...].astype(F32)
+    dst_col = jnp.sum(jnp.where(e_r == e_c, dst_row, 0.0), axis=1, keepdims=True)
+    row_row = row_ref[...].astype(F32)
+    row_col = jnp.sum(jnp.where(e_r == e_c, row_row, 0.0), axis=1, keepdims=True)
+    same = dst_row == dst_col
+    rank_row = jnp.sum(jnp.where(same & (e_r < e_c), 1.0, 0.0), axis=0, keepdims=True)
+    rank_col = jnp.sum(jnp.where(same & (e_c < e_r), 1.0, 0.0), axis=1, keepdims=True)
+    place_row = (dst_row * PACK + rank_row).astype(jnp.int32)
+    place_col = (dst_col * PACK + rank_col).astype(jnp.int32)
+    take = onehot(iota((entries, rows), 1) == row_col.astype(jnp.int32))
+    packed = jnp.zeros((n * PACK, LANE), F32)
+    used = jnp.zeros((n * PACK, entries), F32)
+    slot_iota = iota((n * PACK, entries), 0)
+    for j, ref in enumerate((k_ref, v_ref)):
+        rows_taken = dot(take, ref[...]).astype(BF16)
+        for p in range(pairs):
+            hit = slot_iota == place_row + (2 * p + 8 * j)
+            packed += dot(onehot(hit), rows_taken[:, p * LANE : (p + 1) * LANE])
+            used += jnp.where(hit, 1.0, 0.0)
+    count = jnp.sum(used, axis=1, keepdims=True)
+    packed = jnp.where(count > 0.5, packed, MARK).astype(BF16)
+    ipk[...] = packed.reshape(n, PACK, LANE)
+
+    @pl.loop(1, n)
+    def _(d):
+        peer = lax.rem(me + d, n)
+        iface_copy(ipk, irecv, is_sem, ir_sem, peer, me).start()
+
+    @pl.loop(2, pairs)
+    def _(p):
+        gas_start(p)
+
     live = []
     for b in range(GB):
         mine = block == me * GB + b
@@ -98,90 +204,8 @@
         ]
         bias[s : s + 1, :] = jnp.concatenate(parts + parts, axis=1)
 
-    for i in range(NOFF):
-        for j, ref in enumerate((k_ref, v_ref)):
-            picked = sum(
-                ref[b * BLK : (b + 1) * BLK, :].astype(F32) * picks[i][b] for b in range(GB)
-            ).astype(BF16)
-            for p in range(pairs):
-                gsend[p, i, j] = picked[:, p * LANE : (p + 1) * LANE]
-
-    e_r, e_c = iota((entries, entries), 0), iota((entries, entries), 1)
-    dst_row = dst_ref[...].astype(F32)
-    dst_col = jnp.sum(jnp.where(e_r == e_c, dst_row, 0.0), axis=1, keepdims=True)
-    row_row = row_ref[...].astype(F32)
-    row_col = jnp.sum(jnp.where(e_r == e_c, row_row, 0.0), axis=1, keepdims=True)
-    same = dst_row == dst_col
-    rank_row = jnp.sum(jnp.where(same & (e_r < e_c), 1.0, 0.0), axis=0, keepdims=True)
-    rank_col = jnp.sum(jnp.where(same & (e_c < e_r), 1.0, 0.0), axis=1, keepdims=True)
-    place_row = (dst_row * PACK + rank_row).astype(jnp.int32)
-    place_col = (dst_col * PACK + rank_col).astype(jnp.int32)
-    take = onehot(iota((entries, rows), 1) == row_col.astype(jnp.int32))
-    packed = jnp.zeros((n * PACK, LANE), F32)
-    count = jnp.zeros((n * PACK, 1), F32)
-    slot_iota = iota((n * PACK, entries), 0)
-    for j, ref in enumerate((k_ref, v_ref)):
-        rows_taken = dot(take, ref[...]).astype(BF16)
-        for p in range(pairs):
-            hit = slot_iota == place_row + (2 * p + 8 * j)
-            packed += dot(onehot(hit), rows_taken[:, p * LANE : (p + 1) * LANE])
-            count += jnp.sum(jnp.where(hit, 1.0, 0.0), axis=1, keepdims=True)
-    packed = jnp.where(count > 0.5, packed, MARK).astype(BF16)
-    ipk[...] = packed.reshape(n, PACK, LANE)
-
-    pl.semaphore_wait(barrier, n - 1)
-
-    def gas_copy(p, i):
-        s = rows + i * BLK
-        return pltpu.make_async_remote_copy(
-            src_ref=gsend.at[p, i],
-            dst_ref=kv.at[p, :, pl.ds(s, BLK), :],
-            send_sem=gs_sem.at[p, i],
-            recv_sem=gr_sem.at[p, i],
-            device_id={"space": me + OFFS[i]},
-            device_id_type=MESH,
-        )
-
-    def back_copy(p, i):
-        return pltpu.make_async_remote_copy(
-            src_ref=gback.at[p, i],
-            dst_ref=grecv.at[p, i],
-            send_sem=bs_sem.at[p, i],
-            recv_sem=br_sem.at[p, i],
-            device_id={"space": me - OFFS[i]},
-            device_id_type=MESH,
-        )
-
-    def iface_copy(src, dst, ssem, rsem, peer, slot):
-        return pltpu.make_async_remote_copy(
-            src_ref=src.at[peer],
-            dst_ref=dst.at[slot],
-            send_sem=ssem.at[peer],
-            recv_sem=rsem.at[slot],
-            device_id={"space": peer},
-            device_id_type=MESH,
-        )
-
-    def has(dev):
-        return (dev >= 0) & (dev < n)
-
-    def gas_start(p):
-        for i, off in enumerate(OFFS):
-            @pl.when(has(me + off))
-            def _():
-                gas_copy(p, i).start()
-
-    gas_start(0)
-
-    @pl.loop(1, n)
-    def _(d):
-        peer = lax.rem(me + d, n)
-        iface_copy(ipk, irecv, is_sem, ir_sem, peer, me).start()
-
-    @pl.loop(1, pairs)
-    def _(p):
-        gas_start(p)
-
+    for load in loads[6:]:
+        load.wait()
     irecv[me] = ipk[me]
     for p in range(pairs):
         lanes = slice(p * LANE, (p + 1) * LANE)
@@ -317,15 +341,34 @@
 
         ibrecv[me] = iback[me]
 
-    gas_pair(0)
+    @pl.loop(0, 2)
+    def _(p):
+        gas_pair(p)
+
     melt_all()
 
-    @pl.loop(1, pairs)
+    @pl.loop(2, pairs)
     def _(p):
         gas_pair(p)
 
+    @pl.loop(1, n)
+    def _(d):
+        peer = lax.rem(me + d, n)
+        iface_copy(iback, ibrecv, js_sem, jr_sem, peer, peer).wait_recv()
+
+    flat = ibrecv[...].reshape(n * PACK, LANE)
+    put = onehot(iota((rows, entries), 0) == row_row.astype(jnp.int32))
+    slot_lane = iota((entries, n * PACK), 1)
+
     @pl.loop(0, pairs)
     def _(p):
+        for j in range(2):
+            mine = dot(onehot(slot_lane == place_col + (2 * p + 8 * j)), flat).astype(BF16)
+            own[p, j] += dot(put, mine)
+
+    @pl.loop(0, pairs)
+    def _(p):
+        lanes = pl.ds(pl.multiple_of(p * LANE, LANE), LANE)
         for i, off in enumerate(OFFS):
             @pl.when(has(me + off))
             def _():
@@ -333,19 +376,8 @@
                 got = grecv[p, i].astype(F32)
                 for b in range(GB):
                     own[p, :, b * BLK : (b + 1) * BLK, :] += got * picks[i][b]
-
-    @pl.loop(1, n)
-    def _(d):
-        peer = lax.rem(me + d, n)
-        iface_copy(iback, ibrecv, js_sem, jr_sem, peer, peer).wait_recv()
-
-    flat = ibrecv[...].reshape(n * PACK, LANE)
-    put = onehot(iota((rows, entries), 0) == row_row.astype(jnp.int32))
-    slot_lane = iota((entries, n * PACK), 1)
-    for j, ref in enumerate((dk_ref, dv_ref)):
-        for p in range(pairs):
-            mine = dot(onehot(slot_lane == place_col + (2 * p + 8 * j)), flat).astype(BF16)
-            ref[:, p * LANE : (p + 1) * LANE] = (own[p, j] + dot(put, mine)).astype(BF16)
+        dk_ref[:, lanes] = own[p, 0].astype(BF16)
+        dv_ref[:, lanes] = own[p, 1].astype(BF16)
 
     @pl.loop(0, pairs)
     def _(p):
@@ -363,6 +395,15 @@
         peer = lax.rem(me + d, n)
         iface_copy(ipk, irecv, is_sem, ir_sem, peer, me).wait_send()
         iface_copy(iback, ibrecv, js_sem, jr_sem, peer, me).wait_send()
+
+
+def store(*refs):
+    sems = refs[-1]
+    copies = [pltpu.make_async_copy(refs[i], refs[8 + i], sems.at[i]) for i in range(8)]
+    for copy in copies:
+        copy.start()
+    for copy in copies:
+        copy.wait()
 
 
 def local(n, *args):
@@ -374,16 +415,21 @@
     extra = n * ICAP
     dma = pltpu.SemaphoreType.DMA
     vmem = pl.BlockSpec(memory_space=pltpu.VMEM)
+    ins = (
+        q, k, v, c, ids.T, val.T, if_row.reshape(1, -1), if_dst.reshape(1, -1), mq, mk, mv, mc
+    )
     gas_out = jax.ShapeDtypeStruct((rows, width), BF16)
     melt_out = jax.ShapeDtypeStruct((melt, width), BF16)
     heads = width // HALF
     pieces = heads * (rows * keys + melt * (melt + extra))
-    return pl.pallas_call(
+    outs = pl.pallas_call(
         functools.partial(kernel, n),
         out_shape=[gas_out] * 4 + [melt_out] * 4,
-        in_specs=[vmem] * 12,
+        in_specs=[pl.BlockSpec(memory_space=pltpu.HBM)] * 12,
         out_specs=[vmem] * 8,
         scratch_shapes=[
+            *[pltpu.VMEM(x.shape, x.dtype) for x in ins],
+            dma((len(ins),)),
             pltpu.VMEM((pairs, 2, keys, LANE), BF16),
             pltpu.VMEM((2 * rows, LANE), BF16),
             pltpu.VMEM((2 * rows, LANE), BF16),
@@ -414,14 +460,22 @@
             dma((n,)),
         ],
         compiler_params=pltpu.CompilerParams(
-            collective_id=0, has_side_effects=True, vmem_limit_bytes=48 * 2**20
+            collective_id=0, has_side_effects=True, vmem_limit_bytes=62 * 2**20
         ),
         cost_estimate=pl.CostEstimate(
             flops=pieces * HALF * 10,
             bytes_accessed=16 * width * (rows + melt),
             transcendentals=pieces,
         ),
-    )(q, k, v, c, ids, val, if_row.reshape(1, -1), if_dst.reshape(1, -1), mq, mk, mv, mc)
+    )(*ins)
+    return pl.pallas_call(
+        store,
+        out_shape=[gas_out] * 4 + [melt_out] * 4,
+        in_specs=[vmem] * 8,
+        out_specs=[pl.BlockSpec(memory_space=pltpu.HBM)] * 8,
+        scratch_shapes=[dma((8,))],
+        compiler_params=pltpu.CompilerParams(vmem_limit_bytes=62 * 2**20),
+    )(*outs)
 
 
 def solution(mesh):

time: 70.9 us -> 59.8 us (0.84); the launches traced: 69.8 us -> 59.6 us
  local copies, waits for them, and re-layouts: 14.6 us -> 0 us
  Pallas kernels: 54.5 us -> 58.9 us
    unnamed x32 -> x0, local copies, waits for them, and re-layouts: 14.6 us -> none
    pallas_call x0 -> x1, Pallas kernels: none -> 2.87 us  [local(): pl.pallas_call(store, out_shape=[gas_out] * 4 + [melt_out] * 4, in_specs=...]
    pallas_call x1, Pallas kernels: 54.5 us -> 56 us  [local(): pl.pallas_call(functools.partial(kernel, n), out_shape=[gas_out] * 4 + [m...]
where the time goes in v2:
time: 59.8 us; the launch traced here: 59.6 us
  Pallas kernels  58.9 us (98%)
  between operations  0.65 us (1%)
    pallas_call x1, Pallas kernels, local(): pl.pallas_call(functools.partial(kernel, n), out_shape=[gas_out] * 4 + [m...  56 us
    pallas_call x1, Pallas kernels, local(): pl.pallas_call(store, out_shape=[gas_out] * 4 + [melt_out] * 4, in_specs=...  2.87 us

profile of v2, /device:TPU:0, one launch (start us, length us, event | category | flops | bytes accessed | tf_op | source)
XLA Modules:
  0.0 59.6 jit_solution(16360983303565577776)
XLA Ops:
  0.6 56.0 %shard_map.179 = (bf16[384,512]{1,0:T(8,128)(2,1)}, bf16[384,512]{1,0:T(8,128)(2,1)}, bf16[384,512]{1,0:T(8,128)(2,1)}, bf16[384,512]{1,0:T(8,128)(2,1)}, bf16[1...) custom-call(bf16[384,512]{1,0:T(8,128)(2,1)} %q_hbm.1, ...), custom_call_target="tpu_custom_call" | custom-call | flops 2369781760 | bytes 4194304 | tf_op jit(solution)/shard_map/pallas_call | solution.py:425
  56.7 2.9 %shard_map.180 = (bf16[384,512]{1,0:T(8,128)(2,1)}, bf16[384,512]{1,0:T(8,128)(2,1)}, bf16[384,512]{1,0:T(8,128)(2,1)}, bf16[384,512]{1,0:T(8,128)(2,1)}, bf16[1...) custom-call(bf16[384,512]{1,0:T(8,128)(2,1)} %get-tuple-element.16.refs_0_, ...), custom_call_target="tpu_custom_call" | custom-call | tf_op jit(solution)/shard_map/pallas_call | solution.py:471
